TPU v7x, 512 devices: a whole 4x8x8 slice. The times are simulated.
512 devices in a mesh: src: 16 (over x, z_hi, core), dst: 32 (over y, z_lo).
Axes of the slice: x: 4, y: 8, z: 8 (z_hi: 2, z_lo: 4; z = z_hi * 4 + z_lo), core: 2. Of those that a mesh axis runs over, the one named last changes fastest.
Arguments:
- source_emb: float32 [65536, 400], P(('src', 'dst')), may hold values from -4.5 to 4.5
- dest_emb: float32 [65536, 400], P(('src', 'dst')), may hold values from -4.5 to 4.5
- source_acc: float32 [65536], P(('src', 'dst')), may hold values from 0.01 to 1
- dest_acc: float32 [65536], P(('src', 'dst')), may hold values from 0.01 to 1
- relations: float32 [256, 400], replicated, may hold values from -1 to 1
- rel_acc: float32 [256], replicated, may hold values from 1 to 100
- src_ids: int32 [16, 32, 2, 1000], P('src', 'dst'), may hold values from 0 to 127
- dst_ids: int32 [16, 32, 2, 1000], P('src', 'dst'), may hold values from 0 to 127
- rel_ids: int32 [16, 32, 2, 1000], P('src', 'dst'), may hold values from 0 to 255, as said below
- neg_ids: int32 [16, 32, 2, 1000], P('src', 'dst'), may hold values from 0 to 127
- counts: int32 [16, 32, 2], P('src', 'dst'), may hold values from 125 to 1000
Outputs:
- new_source: float32 [65536, 400], P(('src', 'dst'))
- new_dest: float32 [65536, 400], P(('src', 'dst'))
- new_source_acc: float32 [65536], P(('src', 'dst'))
- new_dest_acc: float32 [65536], P(('src', 'dst'))
- new_relations: float32 [256, 400], replicated
- new_rel_acc: float32 [256], replicated
Inputs may be any that keep to these rules, and one draw needn't show every extreme that they name: `rel_ids`: the relation types of bucket (i, j, s) lie in 8 r to 8 r + 15, taken mod 256, with r = i * 32 + j.
All inputs are finite; a program needn't handle non-finite values.
Results may differ from a plain program's by a relative error of at most 0.0035.
Values may be sent and summed in bfloat16 or wider, within the bound.
A program may use at most 64 MiB of HBM per device.

v0:
```python
import jax
import jax.numpy as jnp
from jax import lax
from jax.sharding import PartitionSpec as P

learn_rate = 0.1


def passed_along(value, axis, steps):
    count = lax.axis_size(axis)
    pairs = [(source, (source + steps) % count) for source in range(count)]
    return lax.ppermute(value, axis, pairs)


def product(left, right, dims):
    return lax.dot_general(left, right, (dims, ((), ())), preferred_element_type=jnp.float32)


def pick_rows(table, index):
    selector = jax.nn.one_hot(index, table.shape[0], dtype=table.dtype)
    return product(selector, table, ((1,), (0,)))


def add_rows(values, index, row_count):
    selector = jax.nn.one_hot(index, row_count, dtype=jnp.float32)
    return lax.dot_general(
        selector,
        values,
        (((0,), (0,)), ((), ())),
        precision=lax.Precision.HIGHEST,
        preferred_element_type=jnp.float32,
    )


def bucket_terms(
    src_block, dst_block, rel_table, src_index, dst_index, rel_index, neg_index, live_count
):
    half_width = src_block.shape[1] // 2
    source_rows = pick_rows(src_block, src_index)
    target_rows = pick_rows(dst_block, dst_index)
    relation_rows = pick_rows(rel_table, rel_index)
    src_real = source_rows[:, :half_width]
    src_imag = source_rows[:, half_width:]
    rel_real = relation_rows[:, :half_width]
    rel_imag = relation_rows[:, half_width:]
    queries = jnp.concatenate(
        [src_real * rel_real - src_imag * rel_imag, src_real * rel_imag + src_imag * rel_real],
        axis=1,
    )
    positive = jnp.sum(queries * target_rows, axis=1)
    query_low = queries.astype(jnp.bfloat16)
    negatives = pick_rows(dst_block, neg_index).astype(jnp.bfloat16)
    scores = product(query_low, negatives, ((1,), (1,)))
    peak_score = jnp.maximum(jnp.max(scores, axis=1), positive)
    pos_weight = jnp.exp(positive - peak_score)
    neg_weight = jnp.exp(scores - peak_score[:, None])
    partition = pos_weight + jnp.sum(neg_weight, axis=1)
    valid_mask = (jnp.arange(scores.shape[0]) < live_count).astype(jnp.float32)
    pos_coeff = valid_mask * (pos_weight / partition - 1.0)
    neg_coeff = ((valid_mask / partition)[:, None] * neg_weight).astype(jnp.bfloat16)
    query_grad = pos_coeff[:, None] * target_rows + product(neg_coeff, negatives, ((1,), (0,)))
    negative_grad = product(neg_coeff, query_low, ((0,), (0,)))
    positive_grad = pos_coeff[:, None] * queries
    grad_real = query_grad[:, :half_width]
    grad_imag = query_grad[:, half_width:]
    source_grad = jnp.concatenate(
        [grad_real * rel_real + grad_imag * rel_imag, grad_imag * rel_real - grad_real * rel_imag],
        axis=1,
    )
    relation_grad = jnp.concatenate(
        [grad_real * src_real + grad_imag * src_imag, grad_imag * src_real - grad_real * src_imag],
        axis=1,
    )
    return (source_grad, positive_grad, negative_grad, relation_grad)


def row_adagrad(table, accum, grad):
    new_accum = accum + jnp.mean(grad * grad, axis=1)
    return (table - learn_rate * grad / jnp.sqrt(new_accum)[:, None], new_accum)


def shards(
    source_emb,
    dest_emb,
    source_acc,
    dest_acc,
    relations,
    rel_acc,
    src_ids,
    dst_ids,
    rel_ids,
    neg_ids,
    counts,
):
    step_count = src_ids.shape[2]
    block_rows = source_emb.shape[0]
    relation_count = relations.shape[0]
    src_index = src_ids.reshape(step_count, -1)
    dst_index = dst_ids.reshape(step_count, -1)
    rel_index = rel_ids.reshape(step_count, -1)
    neg_index = neg_ids.reshape(step_count, -1)
    live_counts = counts.reshape(step_count)
    src_block = source_emb.astype(jnp.bfloat16)
    dst_block = dest_emb.astype(jnp.bfloat16)
    rel_table = relations.astype(jnp.bfloat16)
    source_total = jnp.zeros(source_emb.shape, jnp.float32)
    dest_total = jnp.zeros(dest_emb.shape, jnp.float32)
    relation_total = jnp.zeros(relations.shape, jnp.float32)
    for step_index in range(step_count):
        if step_index > 0:
            src_block = passed_along(src_block, "dst", 1)
            dst_block = passed_along(dst_block, "src", 1)
        source_grad, positive_grad, negative_grad, relation_grad = bucket_terms(
            src_block,
            dst_block,
            rel_table,
            src_index[step_index],
            dst_index[step_index],
            rel_index[step_index],
            neg_index[step_index],
            live_counts[step_index],
        )
        relation_term = add_rows(relation_grad, rel_index[step_index], relation_count)
        relation_total = relation_total + relation_term
        source_rows = src_index[step_index]
        target_rows = jnp.concatenate([dst_index[step_index], neg_index[step_index]])
        target_grad = jnp.concatenate([positive_grad, negative_grad], axis=0)
        source_term = add_rows(source_grad, source_rows, block_rows)
        target_term = add_rows(target_grad, target_rows, block_rows)
        if step_index > 0:
            source_term = passed_along(source_term, "dst", -step_index)
            target_term = passed_along(target_term.astype(jnp.bfloat16), "src", -step_index).astype(
                target_term.dtype
            )
        source_total = source_total + source_term
        dest_total = dest_total + target_term
    new_source, new_source_acc = row_adagrad(source_emb, source_acc, source_total)
    new_dest, new_dest_acc = row_adagrad(dest_emb, dest_acc, dest_total)
    relation_total = lax.psum(relation_total, ("src", "dst"))
    new_relations, new_rel_acc = row_adagrad(relations, rel_acc, relation_total)
    return (new_source, new_dest, new_source_acc, new_dest_acc, new_relations, new_rel_acc)


def solution(mesh):
    in_specs = (
        P(("src", "dst"), None),
        P(("src", "dst"), None),
        P(("src", "dst")),
        P(("src", "dst")),
        P(),
        P(),
        P("src", "dst", None, None),
        P("src", "dst", None, None),
        P("src", "dst", None, None),
        P("src", "dst", None, None),
        P("src", "dst", None),
    )
    out_specs = (
        P(("src", "dst"), None),
        P(("src", "dst"), None),
        P(("src", "dst")),
        P(("src", "dst")),
        P(),
        P(),
    )
    return jax.shard_map(shards, mesh=mesh, in_specs=in_specs, out_specs=out_specs, check_vma=False)
```

profile of v0, /device:TPU:1, one launch (start us, length us, event | category | flops | bytes accessed | tf_op | source)
XLA Modules:
  0.0 344.7 jit_solution(9874634909360793252)
XLA Ops:
  7.2 1.0 convert_element_type.66
  8.2 4.8 %collective-permute-start = (bf16[128,400]{0,1:T(8,128)(2,1)S(1)}, bf16[128,400]{0,1:T(8,128)(2,1)S(1)}, u32[]{:S(2)}, u32[]{:S(2)}) collective-permute-start(bf16[128,400]{0,1:T(8,128)(2,1)S(1)} %convert_element_type.66), channel_id=1, source_target_pairs={{0,1},{1,2},{2,3},{3,4},{4,5},{5,6},{6,7},{7,8},{8,9},{9,10},{10,1... | collective-permute-start | bytes 307208 | tf_op jit(solution)/shard_map/ppermute | solution.py:12
  13.0 0.9 convert_element_type.68
  14.0 10.6 %collective-permute-start.1 = (bf16[128,400]{0,1:T(8,128)(2,1)S(1)}, bf16[128,400]{0,1:T(8,128)(2,1)S(1)}, u32[]{:S(2)}, u32[]{:S(2)}) collective-permute-start(bf16[128,400]{0,1:T(8,128)(2,1)S(1)} %convert_element_type.68), channel_id=1, source_target_pairs={{0,32},{32,64},{64,96},{96,128},{128,160},{160,192},{192,224},{224... | collective-permute-start | bytes 307208 | tf_op jit(solution)/shard_map/ppermute | solution.py:12
  24.6 1.3 fusion.87
  32.1 1.3 fusion.89
  34.7 1.1 fusion.51
  36.1 1.1 multiply_add_fusion.1
  37.2 1.9 multiply_add_fusion.3
  39.1 1.1 fusion.18
  41.8 1.3 fusion.88
  44.9 1.3 fusion.52
  46.5 1.1 multiply_add_fusion
  47.6 0.9 multiply_add_fusion.2
  48.5 1.9 fusion.32
  50.4 1.9 collective-permute-start.3
  52.4 1.7 fusion.14
  54.0 6.4 %collective-permute-start.2 = (f32[128,400]{0,1:T(8,128)}, f32[128,400]{0,1:T(8,128)}, u32[]{:S(2)}, u32[]{:S(2)}) collective-permute-start(f32[128,400]{0,1:T(8,128)} %fusion.14), channel_id=1, source_target_pairs={{0,31},{1,0},{2,1},{3,2},{4,3},{5,4},{6,5},{7,6},{8,7},{9,8},{10,9... | collective-permute-start | bytes 614408 | tf_op jit(solution)/shard_map/ppermute | solution.py:12
  60.4 1.8 fusion.26
  62.3 1.9 multiply_reduce_fusion.3
  65.5 265.6 %all-reduce.2.cloned.1.call-done = f32[256,400]{0,1:T(8,128)} async-done(((f32[256,400]{0,1:T(8,128)}), f32[256,400]{0,1:T(8,128)}) %all-reduce.2.cloned.1.call-update) | async-done | bytes 409616 | tf_op jit(solution)/shard_map/psum | solution.py:139
  331.1 1.1 multiply_reduce_fusion.2
  332.7 2.0 divide_subtract_fusion
  334.7 1.9 multiply_reduce_fusion.4
  (51 shorter events, 14.4 us)
Async XLA Ops:
  7.2 23.0 %copy-start = (f32[256,400]{0,1:T(8,128)S(1)}, f32[256,400]{0,1:T(8,128)}, u32[]{:S(2)}) copy-start(f32[256,400]{0,1:T(8,128)} %param.15) | copy-start | bytes 1228804
  7.2 323.9 %all-reduce.2.cloned.1.call-start = ((), (), s32[]{:S(2)}) async-start(), calls=%async_computation | async-start | bytes 819200 | tf_op jit(solution)/shard_map/psum | solution.py:139
  8.2 32.1 %collective-permute-start = (bf16[128,400]{0,1:T(8,128)(2,1)S(1)}, bf16[128,400]{0,1:T(8,128)(2,1)S(1)}, u32[]{:S(2)}, u32[]{:S(2)}) collective-permute-start(bf16[128,400]{0,1:T(8,128)(2,1)S(1)} %convert_element_type.66), channel_id=1, source_target_pairs={{0,1},{1,2},{2,3},{3,4},{4,5},{5,6},{6,7},{7,8},{8,9},{9,10},{10,1... | collective-permute-start | bytes 307208 | tf_op jit(solution)/shard_map/ppermute | solution.py:12
  14.0 27.3 %collective-permute-start.1 = (bf16[128,400]{0,1:T(8,128)(2,1)S(1)}, bf16[128,400]{0,1:T(8,128)(2,1)S(1)}, u32[]{:S(2)}, u32[]{:S(2)}) collective-permute-start(bf16[128,400]{0,1:T(8,128)(2,1)S(1)} %convert_element_type.68), channel_id=1, source_target_pairs={{0,32},{32,64},{64,96},{96,128},{128,160},{160,192},{192,224},{224... | collective-permute-start | bytes 307208 | tf_op jit(solution)/shard_map/ppermute | solution.py:12
  50.4 11.9 %collective-permute-start.3 = (bf16[128,400]{0,1:T(8,128)(2,1)S(1)}, bf16[128,400]{0,1:T(8,128)(2,1)S(1)}, u32[]{:S(2)}, u32[]{:S(2)}) collective-permute-start(bf16[128,400]{0,1:T(8,128)(2,1)S(1)} %fusion.32), channel_id=1, source_target_pairs={{0,480},{32,0},{64,32},{96,64},{128,96},{160,128},{192,160},{224,1... | collective-permute-start | bytes 307208 | tf_op jit(solution)/shard_map/ppermute | solution.py:12
  54.0 280.6 %collective-permute-start.2 = (f32[128,400]{0,1:T(8,128)}, f32[128,400]{0,1:T(8,128)}, u32[]{:S(2)}, u32[]{:S(2)}) collective-permute-start(f32[128,400]{0,1:T(8,128)} %fusion.14), channel_id=1, source_target_pairs={{0,31},{1,0},{2,1},{3,2},{4,3},{5,4},{6,5},{7,6},{8,7},{9,8},{10,9... | collective-permute-start | bytes 614408 | tf_op jit(solution)/shard_map/ppermute | solution.py:12
  62.3 2.0 copy-start.6
  62.3 2.5 copy-start.3
  62.3 269.8 %copy-start.5 = (f32[256]{0:T(256)S(1)}, f32[256]{0:T(256)}, u32[]{:S(2)}) copy-start(f32[256]{0:T(256)} %param.16) | copy-start | bytes 3076
  64.2 270.5 %copy-start.1 = (f32[1000,200]{0,1:T(8,128)S(1)}, f32[1000,200]{0,1:T(8,128)}, u32[]{:S(2)}) copy-start(f32[1000,200]{0,1:T(8,128)} %get-tuple-element.26) | copy-start | bytes 2400004
  64.2 270.4 %copy-start.2 = (f32[1000,200]{0,1:T(8,128)S(1)}, f32[1000,200]{0,1:T(8,128)}, u32[]{:S(2)}) copy-start(f32[1000,200]{0,1:T(8,128)} %get-tuple-element.27) | copy-start | bytes 2400004
  332.7 3.9 %copy-start.7 = (f32[128]{0:T(128)S(1)}, f32[128]{0:T(128)}, u32[]{:S(2)}) copy-start(f32[128]{0:T(128)} %param.13) | copy-start | bytes 1540
  332.7 4.4 %copy-start.4 = (f32[128,400]{0,1:T(8,128)S(1)}, f32[128,400]{0,1:T(8,128)}, u32[]{:S(2)}) copy-start(f32[128,400]{0,1:T(8,128)} %param.11) | copy-start | bytes 614404
Sparse Core Ops, SparseCore 0:
  62.4 268.6 all-reduce.1
where the time goes:
time: 345 us
  waiting for transfers between devices  266 us (77%)
  starting transfers between devices  23.7 us (7%)
  matrix products  21.6 us (6%)
  other arithmetic  15 us (4%)
  between operations  14.4 us (4%)
  local copies, waits for them, and re-layouts  4.48 us (1%)
    psum x1, waiting for transfers between devices, shards(): relation_total = lax.psum(relation_total, ('src', 'dst'))  266 us
    ppermute x4, starting transfers between devices, passed_along(): return lax.ppermute(value, axis, pairs)  23.7 us
    dot_general x14, matrix products, product(): lax.dot_general(left, right, (dims, ((), ())), preferred_element_type=jnp...  11.3 us
    dot_general x6, matrix products, add_rows(): lax.dot_general(selector, values, (((0,), (0,)), ((), ())), precision=lax...  10.3 us
  transfers between devices with their start and end apart: 5, of which 1 were waited for; matrix products, arithmetic and copies ran while one was open for 8% of the time, Pallas kernels for 0%

commit v1 on v0

v1 whole, which is shorter than its diff:
```python
import functools

import jax
import jax.numpy as jnp
from jax import lax
from jax.experimental import pallas as pl
from jax.experimental.pallas import tpu as pltpu
from jax.sharding import PartitionSpec as P

MESH = pl.DeviceIdType.MESH
F32 = jnp.float32
BF16 = jnp.bfloat16
learn_rate = 0.1

ZH, ZL, NC = 2, 4, 2
LANES = 128
CHUNK = 256
ABSENT = -1e30


def split2(value):
    high = value.astype(BF16)
    low = (value - high.astype(F32)).astype(BF16)
    return high, low


def nn(left, right):
    return jnp.dot(left, right, preferred_element_type=F32)


def nt(left, right):
    return lax.dot_general(left, right, (((1,), (1,)), ((), ())), preferred_element_type=F32)


def kernel(
    NX,
    NY,
    counts,
    source_emb,
    dest_emb,
    source_acc,
    dest_acc,
    relations,
    rel_acc,
    src_ids,
    dst_ids,
    rel_ids,
    neg_ids,
    new_source,
    new_dest,
    new_source_acc,
    new_dest_acc,
    new_relations,
    new_rel_acc,
    ids,
    src_t,
    dst_t,
    dst_n,
    rel_t,
    count_b,
    query_s,
    weight_s,
    grad_s,
    rel_sum,
    src_sum,
    dst_sum,
    back_out,
    back_in,
    turn,
    acc_b,
    part,
    part_in,
    mine,
    column,
    full,
    x_send,
    x_recv,
    b_send,
    b_recv,
    s1_send,
    s1_recv,
    s2_send,
    s2_recv,
    s3_send,
    s3_recv,
    s4_send,
    s4_recv,
    s5_send,
    s5_recv,
):
    emb = source_emb.shape[1]
    half = emb // 2
    slots = src_ids.shape[1]
    chunks = pl.cdiv(slots, CHUNK)
    tail = slots - (chunks - 1) * CHUNK
    n_src, n_dst = NX * ZH * NC, NY * ZL
    rel_count = relations.shape[0]
    blocks = [(b * LANES, min(LANES, emb - b * LANES)) for b in range(NX)]

    i = lax.axis_index("src")
    j = lax.axis_index("dst")
    x, zh, c = i // (ZH * NC), (i // NC) % ZH, i % NC
    y, zl = j // ZL, j % ZL

    def place(x, zh, c, y, zl):
        return ((x * ZH + zh) * NC + c, y * ZL + zl)

    def wrap(value, size):
        return lax.rem(value, size)

    ring_next = ((i, wrap(j + 1, n_dst)), (wrap(i + 1, n_src), j))
    ring_prev = ((i, wrap(j + n_dst - 1, n_dst)), (wrap(i + n_src - 1, n_src), j))
    s1_steps = [(dx, dc) for dx in range(NX) for dc in range(NC) if dx or dc]
    s1_peers = [place(wrap(x + dx, NX), zh, wrap(c + dc, NC), y, zl) for dx, dc in s1_steps]
    s2_steps = [(dh, dl, dc) for dh in range(ZH) for dl in range(ZL) for dc in range(NC)]
    special = jnp.logical_and(zl == ZL - 1, c == 1)
    far_y = jnp.where(special, wrap(y + 1, NY), y)

    def s2_peer(step, at_y):
        dh, dl, dc = step
        return place(x, wrap(zh + dh, ZH), wrap(c + dc, NC), at_y, wrap(zl + dl, ZL))

    s3_peers = [place(x, zh, c, wrap(y + dy, NY), zl) for dy in range(1, NY)]
    s4_peers = [place(wrap(x + dx, NX), zh, c, y, zl) for dx in range(1, NX)]
    sibling = place(x, zh, 1 - c, y, zl)

    barrier = pltpu.get_barrier_semaphore()
    greeted = list(ring_next) + list(ring_prev) + s1_peers + s3_peers
    greeted += [s2_peer(step, y) for step in s2_steps[1:]]
    expected = len(greeted)
    before_y = wrap(y + NY - 1, NY)
    greeted += [place(x, h, 1, before_y, ZL - 1) for h in range(ZH)]
    for peer in greeted:
        pl.semaphore_signal(barrier, inc=1, device_id=peer, device_id_type=MESH)

    def turned(block):
        width = block.shape[1]
        if width < LANES:
            block = jnp.concatenate([block, jnp.zeros((block.shape[0], LANES - width), F32)], axis=1)
        return block.T[:width]

    for start, width in blocks:
        src_t[0, start : start + width, :] = turned(source_emb[:, start : start + width]).astype(BF16)
        dst_t[0, start : start + width, :] = turned(dest_emb[:, start : start + width]).astype(BF16)
    dst_n[0, :, :] = dest_emb[...].astype(BF16)

    pl.semaphore_wait(barrier, jnp.where(special, expected + ZH * ZL * NC, expected))

    def remote(src, dst, send, recv, peer):
        return pltpu.make_async_remote_copy(
            src_ref=src, dst_ref=dst, send_sem=send, recv_sem=recv, device_id=peer, device_id_type=MESH
        )

    give_src = remote(src_t.at[0], src_t.at[1], x_send.at[0], x_recv.at[0], ring_next[0])
    give_dst = remote(dst_t.at[0], dst_t.at[1], x_send.at[1], x_recv.at[1], ring_next[1])
    give_src.start()
    give_dst.start()

    first = pl.multiple_of(j * 8, 8)
    second = pl.multiple_of(wrap(j + 1, n_dst) * 8, 8)
    rel_rows = jnp.concatenate(
        [relations[pl.ds(first, 8), :], relations[pl.ds(second, 8), :], jnp.zeros((LANES - 16, emb), F32)], axis=0
    )
    for start, width in blocks:
        rel_t[start : start + width, :] = turned(rel_rows[:, start : start + width]).astype(BF16)

    ids[...] = jnp.full(ids.shape, -1, jnp.int32)
    for s in range(2):
        for n, table in enumerate((src_ids, dst_ids, rel_ids, neg_ids)):
            for q in range(chunks):
                width = CHUNK if q < chunks - 1 else tail
                row = table[s : s + 1, q * CHUNK : q * CHUNK + width]
                if n == 2:
                    row = jnp.bitwise_and(row - 8 * j, rel_count - 1)
                ids[s * chunks + q, n : n + 1, 0:width] = row

    iota = lax.broadcasted_iota(jnp.int32, (LANES, CHUNK), 0)
    lane = lax.broadcasted_iota(jnp.int32, (1, CHUNK), 1)

    for s in range(2):
        seen = jnp.zeros((LANES, CHUNK), F32)
        for q in range(chunks):
            seen = seen + jnp.where(iota == ids[s * chunks + q, 3:4, :], 1.0, 0.0)
        count_b[s] = jnp.broadcast_to(jnp.sum(seen, axis=1, keepdims=True), (LANES, CHUNK))

    rel_sum[...] = jnp.zeros(rel_sum.shape, F32)
    src_sum[...] = jnp.zeros(src_sum.shape, F32)
    dst_sum[...] = jnp.zeros(dst_sum.shape, F32)
    turn[...] = jnp.zeros(turn.shape, F32)
    wide = min(LANES, rel_count)
    for b in range(rel_count // wide):
        row = rel_acc[0:1, b * wide : (b + 1) * wide]
        acc_b[b * wide : (b + 1) * wide, :] = jnp.broadcast_to(row, (LANES, wide)).T

    def first_pass(s):
        live_count = counts[s]

        def body(local, carry):
            q = s * chunks + local
            rows = ids[q]
            one_src = jnp.where(iota == rows[0:1], 1.0, 0.0).astype(BF16)
            hit_dst = iota == rows[1:2]
            one_rel = jnp.where(iota == rows[2:3], 1.0, 0.0).astype(BF16)
            a = nn(src_t[s], one_src)
            r = nn(rel_t[...], one_rel)
            a_re, a_im, r_re, r_im = a[:half], a[half:], r[:half], r[half:]
            query = jnp.concatenate([a_re * r_re - a_im * r_im, a_re * r_im + a_im * r_re], axis=0)
            query_high, query_low = split2(query)
            scores = nn(dst_n[s], query_high)
            rest = nn(dst_n[s], query_low)
            positive = jnp.sum(jnp.where(hit_dst, scores + rest, 0.0), axis=0, keepdims=True)
            seen = count_b[s]
            scores = jnp.where(seen > 0.0, scores, ABSENT)
            peak = jnp.maximum(jnp.max(scores, axis=0, keepdims=True), positive)
            pos_weight = jnp.exp(positive - peak)
            neg_weight = jnp.exp(scores - peak)
            partition = pos_weight + jnp.sum(neg_weight * seen, axis=0, keepdims=True)
            live = jnp.where(lane + local * CHUNK < live_count, 1.0, 0.0)
            pos_coeff = live * (pos_weight / partition - 1.0)
            neg_coeff = (neg_weight * (live / partition)).astype(BF16).astype(F32)
            pos_part = jnp.where(hit_dst, pos_coeff, 0.0)
            weight_high, weight_low = split2(neg_coeff * seen + pos_part)
            query_s[q, 0] = query_high
            query_s[q, 1] = query_low
            weight_s[q, 0] = weight_high
            weight_s[q, 1] = weight_low
            weight_s[q, 2] = pos_part.astype(BF16)
            table = dst_t[s]
            g = nn(
                jnp.concatenate([table, table], axis=1),
                jnp.concatenate([weight_high, weight_low], axis=0),
            )
            g_re, g_im = g[:half], g[half:]
            rel_grad = jnp.concatenate([g_re * a_re + g_im * a_im, g_im * a_re - g_re * a_im], axis=0)
            rel_high, rel_low = split2(rel_grad)
            rel_sum[0:emb, :] += nt(rel_high, one_rel) + nt(rel_low, one_rel)
            src_grad = jnp.concatenate([g_re * r_re + g_im * r_im, g_im * r_re - g_re * r_im], axis=0)
            src_high, src_low = split2(src_grad)
            grad_s[q, 0] = src_high
            grad_s[q, 1] = src_low
            return carry

        lax.fori_loop(0, chunks, body, 0)

    def second_pass(s):
        def body(local, carry):
            q = s * chunks + local
            rows = ids[q]
            one_src = jnp.where(iota == rows[0:1], 1.0, 0.0).astype(BF16)
            src_sum[s] += nt(grad_s[q, 0], one_src) + nt(grad_s[q, 1], one_src)
            dst_sum[s] += (
                nt(query_s[q, 0], weight_s[q, 0])
                + nt(query_s[q, 0], weight_s[q, 1])
                + nt(query_s[q, 1], weight_s[q, 2])
            )
            return carry

        lax.fori_loop(0, chunks, body, 0)

    first_pass(0)
    give_src.wait()
    give_dst.wait()
    for start, width in blocks:
        block = dst_t[1, start : start + width, :].astype(F32)
        if width < LANES:
            block = jnp.concatenate([block, jnp.zeros((LANES - width, LANES), F32)], axis=0)
        dst_n[1, :, start : start + width] = block.T[:, :width].astype(BF16)
    first_pass(1)

    for b in range(NX):
        block = rel_sum[b * LANES : (b + 1) * LANES, :].T
        for rows in range(NC):
            part[b, rows] = block[8 * rows : 8 * rows + 8, :]
    s1 = [
        remote(
            part.at[wrap(x + dx, NX), wrap(c + dc, NC)],
            part_in.at[n],
            s1_send.at[n],
            s1_recv.at[n],
            s1_peers[n],
        )
        for n, (dx, dc) in enumerate(s1_steps)
    ]
    for copy in s1:
        copy.start()

    second_pass(1)
    back_out[0] = src_sum[1].astype(BF16)
    back_out[1] = dst_sum[1].astype(BF16)
    back = [remote(back_out.at[n], back_in.at[n], b_send.at[n], b_recv.at[n], ring_prev[n]) for n in range(2)]
    for copy in back:
        copy.start()

    tile = part[x, c]
    for n, copy in enumerate(s1):
        copy.wait()
        tile = tile + part_in[n]
    mine[...] = tile

    s2 = [
        remote(mine, column.at[zh, zl, c], s2_send.at[n], s2_recv.at[n], s2_peer(step, far_y))
        for n, step in enumerate(s2_steps)
    ]
    for copy in s2[1:]:
        copy.start()

    @pl.when(special)
    def _():
        s2[0].start()

    @pl.when(jnp.logical_not(special))
    def _():
        column[zh, zl, c] = mine[...]

    second_pass(0)
    for copy in s2[1:]:
        copy.wait()

    @pl.when(special)
    def _():
        s2[0].wait()

    firsts = [column[0, l, 0] + column[1, l, 0] for l in range(ZL)]
    lasts = [column[0, l, 1] + column[1, l, 1] for l in range(ZL)]
    whole = [firsts[l] + lasts[(l + ZL - 1) % ZL] for l in range(ZL)]
    for n in range(2):
        full[x, y, c, n] = jnp.where(c == 0, whole[n], whole[2 + n])
    order = sorted(range(NY), key=lambda dy: (min(dy, NY - dy), dy))
    s3 = {
        dy: remote(full.at[x, y, c], full.at[x, y, c], s3_send.at[dy], s3_recv.at[dy], s3_peers[dy - 1])
        for dy in order
        if dy
    }
    for dy in order[1:]:
        s3[dy].start()

    def s4_copies(dy):
        at = full.at[x, wrap(y + NY - dy, NY), c]
        return [
            remote(at, at, s4_send.at[dy, n], s4_recv.at[dy, n], s4_peers[n]) for n in range(NX - 1)
        ]

    def s5_copy(dy):
        at = full.at[:, wrap(y + NY - dy, NY), c]
        return remote(at, at, s5_send.at[dy], s5_recv.at[dy], sibling)

    s4 = {dy: s4_copies(dy) for dy in order}
    s5 = {dy: s5_copy(dy) for dy in order}
    for copy in s4[0]:
        copy.start()

    def update(n, sums, table, acc, out, new_acc):
        back[n].wait()
        total = sums[0] + back_in[n].astype(F32)
        accum = acc[...] + jnp.sum(total * total, axis=0, keepdims=True) * (1.0 / emb)
        new_acc[...] = accum
        turn[0:emb, :] = total * (learn_rate / jnp.sqrt(accum))
        for b, (start, width) in enumerate(blocks):
            step = turn[b * LANES : (b + 1) * LANES, :].T
            out[:, start : start + width] = table[:, start : start + width] - step[:, :width]

    update(0, src_sum, source_emb, source_acc, new_source, new_source_acc)
    update(1, dst_sum, dest_emb, dest_acc, new_dest, new_dest_acc)

    def to_sibling(dy):
        for copy in s4[dy]:
            copy.wait_recv()
        s5[dy].start()

    lag = 3
    for n, dy in enumerate(order):
        if dy:
            s3[dy].wait_recv()
            for copy in s4[dy]:
                copy.start()
        if n >= lag:
            to_sibling(order[n - lag])
    for dy in order[max(0, NY - lag) :]:
        to_sibling(dy)
    for dy in order:
        s5[dy].wait_recv()

    tiles = [full[b].reshape(rel_count, LANES) for b in range(NX)]
    squares = tiles[0] * tiles[0]
    for tile in tiles[1:]:
        squares = squares + tile * tile
    accum = acc_b[...] + jnp.sum(squares, axis=1, keepdims=True) * (1.0 / emb)
    scale = learn_rate / jnp.sqrt(accum)
    for b, (start, width) in enumerate(blocks):
        step = tiles[b] * scale
        new_relations[:, start : start + width] = relations[:, start : start + width] - step[:, :width]
    for b in range(rel_count // wide):
        block = accum[b * wide : (b + 1) * wide, :].T
        new_rel_acc[0:1, b * wide : (b + 1) * wide] = block[0:1, :]

    for dy in order:
        if dy:
            s3[dy].wait_send()
        for copy in s4[dy]:
            copy.wait_send()
        s5[dy].wait_send()


def solution(mesh):
    n_src, n_dst = mesh.shape["src"], mesh.shape["dst"]
    NX, NY = n_src // (ZH * NC), n_dst // ZL

    def shards(
        source_emb,
        dest_emb,
        source_acc,
        dest_acc,
        relations,
        rel_acc,
        src_ids,
        dst_ids,
        rel_ids,
        neg_ids,
        counts,
    ):
        rows, emb = source_emb.shape
        rel_count = relations.shape[0]
        slots = src_ids.shape[3]
        chunks = pl.cdiv(slots, CHUNK)
        vmem = pl.BlockSpec(memory_space=pltpu.VMEM)
        smem = pl.BlockSpec(memory_space=pltpu.SMEM)
        dma = pltpu.SemaphoreType.DMA
        outs = pl.pallas_call(
            functools.partial(kernel, NX, NY),
            out_shape=(
                jax.ShapeDtypeStruct((rows, emb), F32),
                jax.ShapeDtypeStruct((rows, emb), F32),
                jax.ShapeDtypeStruct((1, rows), F32),
                jax.ShapeDtypeStruct((1, rows), F32),
                jax.ShapeDtypeStruct((rel_count, emb), F32),
                jax.ShapeDtypeStruct((1, rel_count), F32),
            ),
            in_specs=[smem] + [vmem] * 10,
            out_specs=[vmem] * 6,
            scratch_shapes=[
                pltpu.VMEM((2 * chunks, 4, CHUNK), jnp.int32),
                pltpu.VMEM((2, emb, LANES), BF16),
                pltpu.VMEM((2, emb, LANES), BF16),
                pltpu.VMEM((2, LANES, emb), BF16),
                pltpu.VMEM((emb, LANES), BF16),
                pltpu.VMEM((2, LANES, CHUNK), F32),
                pltpu.VMEM((2 * chunks, 2, emb, CHUNK), BF16),
                pltpu.VMEM((2 * chunks, 3, LANES, CHUNK), BF16),
                pltpu.VMEM((2 * chunks, 2, emb, CHUNK), BF16),
                pltpu.VMEM((NX * LANES, LANES), F32),
                pltpu.VMEM((2, emb, LANES), F32),
                pltpu.VMEM((2, emb, LANES), F32),
                pltpu.VMEM((2, emb, LANES), BF16),
                pltpu.VMEM((2, emb, LANES), BF16),
                pltpu.VMEM((NX * LANES, LANES), F32),
                pltpu.VMEM((rel_count, LANES), F32),
                pltpu.VMEM((NX, NC, 8, LANES), F32),
                pltpu.VMEM((NX * NC - 1, 8, LANES), F32),
                pltpu.VMEM((8, LANES), F32),
                pltpu.VMEM((ZH, ZL, NC, 8, LANES), F32),
                pltpu.VMEM((NX, NY, NC, ZL // NC, 8, LANES), F32),
                dma((2,)),
                dma((2,)),
                dma((2,)),
                dma((2,)),
                dma((NX * NC - 1,)),
                dma((NX * NC - 1,)),
                dma((ZH * ZL * NC,)),
                dma((ZH * ZL * NC,)),
                dma((NY,)),
                dma((NY,)),
                dma((NY, NX - 1)),
                dma((NY, NX - 1)),
                dma((NY,)),
                dma((NY,)),
            ],
            compiler_params=pltpu.CompilerParams(
                collective_id=0, has_side_effects=True, vmem_limit_bytes=40 * 2**20
            ),
            cost_estimate=pl.CostEstimate(flops=4 * 10**9, bytes_accessed=3 * 10**6, transcendentals=3 * 10**5),
            name="bucket_round",
        )(
            counts.reshape(2),
            source_emb,
            dest_emb,
            source_acc.reshape(1, rows),
            dest_acc.reshape(1, rows),
            relations,
            rel_acc.reshape(1, rel_count),
            src_ids.reshape(2, slots),
            dst_ids.reshape(2, slots),
            rel_ids.reshape(2, slots),
            neg_ids.reshape(2, slots),
        )
        new_source, new_dest, new_source_acc, new_dest_acc, new_relations, new_rel_acc = outs
        return (
            new_source,
            new_dest,
            new_source_acc.reshape(rows),
            new_dest_acc.reshape(rows),
            new_relations,
            new_rel_acc.reshape(rel_count),
        )

    rows_spec = P(("src", "dst"), None)
    row_spec = P(("src", "dst"))
    ids_spec = P("src", "dst", None, None)
    return jax.shard_map(
        shards,
        mesh=mesh,
        in_specs=(rows_spec, rows_spec, row_spec, row_spec, P(), P())
        + (ids_spec,) * 4
        + (P("src", "dst", None),),
        out_specs=(rows_spec, rows_spec, row_spec, row_spec, P(), P()),
        check_vma=False,
    )
```

time: 345 us -> 58.3 us (0.17)
  waiting for transfers between devices: 266 us -> 0 us
  Pallas kernels: 0 us -> 51.2 us
  starting transfers between devices: 23.7 us -> 0 us
  matrix products: 21.6 us -> 0 us
  other arithmetic: 15 us -> 0 us
  between operations: 14.4 us -> 0.77 us
    psum x1 -> x0, waiting for transfers between devices: 266 us -> none  [shards(): relation_total = lax.psum(relation_total, ('src', 'dst'))]
    pallas_call x0 -> x1, Pallas kernels: none -> 51.2 us  [shards(): pl.pallas_call(functools.partial(kernel, NX, NY), out_shape=(jax.ShapeDty...]
    ppermute x4 -> x0, starting transfers between devices: 23.7 us -> none  [passed_along(): return lax.ppermute(value, axis, pairs)]
    dot_general x20 -> x0, matrix products: 21.6 us -> none  [the longest x14 11.3 us: product(): lax.dot_general(left, right, (dims, ((), ())), preferred_element_type=jnp...]
    unnamed x16 -> x29, local copies, waits for them, and re-layouts: 0.04 us -> 6.09 us
    slice x5 -> x0, local copies, waits for them, and re-layouts: 4.44 us -> none  [the longest x1 1.31 us: shards(): live_counts[step_index]]
    sub x5 -> x0, other arithmetic: 4.33 us -> none  [the longest x3 3.41 us: row_adagrad(): return (table - learn_rate * grad / jnp.sqrt(new_accum)[:, None], new_accum)]
  transfers between devices with their start and end apart: 5 -> 0, of which waited for: 1 -> 0; matrix products, arithmetic and copies ran while one was open for 8% -> 0% of each run, Pallas kernels for 0% -> 0%
where the time goes in v1:
time: 58.3 us; the launch traced here: 58.1 us
  Pallas kernels  51.2 us (88%)
  local copies, waits for them, and re-layouts  6.09 us (10%)
  between operations  0.77 us (1%)
    pallas_call x1, Pallas kernels, shards(): pl.pallas_call(functools.partial(kernel, NX, NY), out_shape=(jax.ShapeDty...  51.2 us
    unnamed x29, local copies, waits for them, and re-layouts  6.09 us

profile of v1, /device:TPU:1, one launch (start us, length us, event | category | flops | bytes accessed | tf_op | source)
XLA Modules:
  0.0 58.1 jit_solution(5113099989689628879)
XLA Ops:
  0.7 1.1 %copy.17.source_emb = f32[128,400]{1,0:T(8,128)S(1)} copy(f32[128,400]{0,1:T(8,128)} %param.11) | data formatting | bytes 409600 | tf_op args[0]
  1.8 0.1 copy.18.dest_emb
  1.9 0.0 copy-done.8
  1.9 0.0 copy-start
  1.9 0.0 copy-start.1
  2.0 0.0 copy-start.2
  2.0 0.0 copy-start.3
  2.0 0.0 copy-start.4
  2.0 0.0 copy-start.5
  2.0 0.0 copy-start.6
  2.0 0.0 copy-start.7
  2.0 0.2 copy.19.relations
  2.2 0.4 copy-done
  2.6 0.0 copy-done.1
  2.7 0.0 copy-done.2
  2.7 0.0 copy-done.3
  2.7 0.0 copy-done.7
  2.7 51.2 %bucket_round.1 = (f32[128,400]{1,0:T(8,128)S(1)}, f32[128,400]{1,0:T(8,128)S(1)}, f32[1,128]{1,0:T(1,128)S(1)}, f32[1,128]{1,0:T(1,128)S(1)}, f32[256,400]{1,0:T(8,128)S(1)}, /*index=5*/f32[1,256]{1,0:T(1,128)S(1)}) custom-call(s32[2]{0:T(128)S(1)} %bitcast.17, f32[128,400]{1,0:T(8,128)S(1)} %copy.17.source_emb, f32[128,400]{1,0:T(8,128)S(1)} %copy.18.dest_emb, ...), custom_call_target="tpu_custom_call" | custom-call | flops 4000000000 | bytes 3000000 | tf_op jit(solution)/shard_map/bucket_round/pallas_call | solution.py:428
  54.0 0.8 %copy.20 = f32[128,400]{0,1:T(8,128)} copy(f32[128,400]{1,0:T(8,128)S(1)} %get-tuple-element.18) | data formatting | bytes 409600
  54.8 0.8 %copy.21 = f32[128,400]{0,1:T(8,128)} copy(f32[128,400]{1,0:T(8,128)S(1)} %get-tuple-element.19) | data formatting | bytes 409600
  55.6 0.9 %copy.22 = f32[256,400]{0,1:T(8,128)} copy(f32[256,400]{1,0:T(8,128)S(1)} %get-tuple-element.22) | data formatting | bytes 819200
  56.5 0.5 copy.26
  57.0 0.5 copy.27
  57.5 0.6 copy.28
  (6 shorter events, 0.0 us)
Async XLA Ops:
  0.6 1.1 %copy-start.9 = (f32[128,400]{0,1:T(8,128)S(1)}, f32[128,400]{0,1:T(8,128)}, u32[]{:S(2)}) copy-start(f32[128,400]{0,1:T(8,128)} %param.12) | copy-start | bytes 614404
  0.6 1.3 %copy-start.8 = (f32[256,400]{0,1:T(8,128)S(1)}, f32[256,400]{0,1:T(8,128)}, u32[]{:S(2)}) copy-start(f32[256,400]{0,1:T(8,128)} %param.15) | copy-start | bytes 1228804
  1.9 0.7 %copy-start = (s32[1,1,2,1000]{3,2,1,0:T(2,128)S(1)}, s32[1,1,2,1000]{3,2,1,0:T(2,128)}, u32[]{:S(2)}) copy-start(s32[1,1,2,1000]{3,2,1,0:T(2,128)} %param.17) | copy-start | bytes 24004
  1.9 0.7 %copy-start.1 = (s32[1,1,2,1000]{3,2,1,0:T(2,128)S(1)}, s32[1,1,2,1000]{3,2,1,0:T(2,128)}, u32[]{:S(2)}) copy-start(s32[1,1,2,1000]{3,2,1,0:T(2,128)} %param.18) | copy-start | bytes 24004
  2.0 0.7 %copy-start.2 = (s32[1,1,2,1000]{3,2,1,0:T(2,128)S(1)}, s32[1,1,2,1000]{3,2,1,0:T(2,128)}, u32[]{:S(2)}) copy-start(s32[1,1,2,1000]{3,2,1,0:T(2,128)} %param.19) | copy-start | bytes 24004
  2.0 0.7 %copy-start.3 = (s32[1,1,2,1000]{3,2,1,0:T(2,128)S(1)}, s32[1,1,2,1000]{3,2,1,0:T(2,128)}, u32[]{:S(2)}) copy-start(s32[1,1,2,1000]{3,2,1,0:T(2,128)} %param.20) | copy-start | bytes 24004
  2.0 0.7 %copy-start.4 = (f32[256]{0:T(256)S(1)}, f32[256]{0:T(256)}, u32[]{:S(2)}) copy-start(f32[256]{0:T(256)} %param.16) | copy-start | bytes 3076
  2.0 0.7 %copy-start.5 = (s32[1,1,2]{2,1,0:T(1,128)S(1)}, s32[1,1,2]{2,1,0:T(1,128)}, u32[]{:S(2)}) copy-start(s32[1,1,2]{2,1,0:T(1,128)} %param.21) | copy-start | bytes 28
  2.0 0.7 %copy-start.6 = (f32[128]{0:T(128)S(1)}, f32[128]{0:T(128)}, u32[]{:S(2)}) copy-start(f32[128]{0:T(128)} %param.13) | copy-start | bytes 1540
  2.0 0.7 %copy-start.7 = (f32[128]{0:T(128)S(1)}, f32[128]{0:T(128)}, u32[]{:S(2)}) copy-start(f32[128]{0:T(128)} %param.14) | copy-start | bytes 1540

commit v2 on v1

v2 whole, which is shorter than its diff:
```python
import functools

import jax
import jax.numpy as jnp
from jax import lax
from jax.experimental import pallas as pl
from jax.experimental.pallas import tpu as pltpu
from jax.sharding import PartitionSpec as P

MESH = pl.DeviceIdType.MESH
F32 = jnp.float32
BF16 = jnp.bfloat16
learn_rate = 0.1

ZH, ZL, NC = 2, 4, 2
LANES = 128
CHUNK = 256
ABSENT = -1e30


def split2(value):
    high = value.astype(BF16)
    low = (value - high.astype(F32)).astype(BF16)
    return high, low


def nn(left, right):
    return jnp.dot(left, right, preferred_element_type=F32)


def nt(left, right):
    return lax.dot_general(left, right, (((1,), (1,)), ((), ())), preferred_element_type=F32)


def kernel(
    NX,
    NY,
    counts_hbm,
    source_emb_hbm,
    dest_emb_hbm,
    source_acc_hbm,
    dest_acc_hbm,
    relations_hbm,
    rel_acc_hbm,
    src_ids_hbm,
    dst_ids_hbm,
    rel_ids_hbm,
    neg_ids_hbm,
    new_source,
    new_dest,
    new_source_acc,
    new_dest_acc,
    new_relations,
    new_rel_acc,
    counts,
    source_emb,
    dest_emb,
    source_acc,
    dest_acc,
    relations,
    rel_acc,
    src_ids,
    dst_ids,
    rel_ids,
    neg_ids,
    ids,
    src_t,
    dst_t,
    dst_n,
    rel_t,
    count_b,
    query_s,
    weight_s,
    grad_s,
    rel_sum,
    src_sum,
    dst_sum,
    back_out,
    back_in,
    part,
    part_in,
    mine,
    column,
    full,
    in_sem,
    x_send,
    x_recv,
    b_send,
    b_recv,
    s1_send,
    s1_recv,
    s2_send,
    s2_recv,
    s3_send,
    s3_recv,
    s4_send,
    s4_recv,
    s5_send,
    s5_recv,
):
    loads = [
        pltpu.make_async_copy(src, dst, in_sem.at[n])
        for n, (src, dst) in enumerate(
            (
                (counts_hbm, counts),
                (rel_ids_hbm, rel_ids),
                (src_ids_hbm, src_ids),
                (dst_ids_hbm, dst_ids),
                (neg_ids_hbm, neg_ids),
                (source_emb_hbm, source_emb),
                (dest_emb_hbm, dest_emb),
                (relations_hbm, relations),
                (source_acc_hbm, source_acc),
                (dest_acc_hbm, dest_acc),
                (rel_acc_hbm, rel_acc),
            )
        )
    ]
    for load in loads:
        load.start()

    emb = source_emb.shape[0]
    half = emb // 2
    slots = src_ids.shape[1]
    chunks = pl.cdiv(slots, CHUNK)
    tail = slots - (chunks - 1) * CHUNK
    n_src, n_dst = NX * ZH * NC, NY * ZL
    rel_count = relations.shape[1]
    blocks = [(b * LANES, min(LANES, emb - b * LANES)) for b in range(NX)]

    i = lax.axis_index("src")
    j = lax.axis_index("dst")
    x, zh, c = i // (ZH * NC), jnp.bitwise_and(i // NC, ZH - 1), jnp.bitwise_and(i, NC - 1)
    y, zl = j // ZL, jnp.bitwise_and(j, ZL - 1)

    def place(x, zh, c, y, zl):
        return ((x * ZH + zh) * NC + c, y * ZL + zl)

    def wrap(value, size):
        return jnp.bitwise_and(value, size - 1)

    i_up, i_down = wrap(i + 1, n_src), wrap(i + n_src - 1, n_src)
    j_up, j_down = wrap(j + 1, n_dst), wrap(j + n_dst - 1, n_dst)
    ring = [(i_down, j), (i_up, j), (i_down, j_up), (i_up, j_down)]
    s1_steps = [(dx, dc) for dx in range(NX) for dc in range(NC) if dx or dc]
    s1_peers = [place(wrap(x + dx, NX), zh, wrap(c + dc, NC), y, zl) for dx, dc in s1_steps]
    s2_steps = [(dh, dl, dc) for dh in range(ZH) for dl in range(ZL) for dc in range(NC)]
    special = jnp.logical_and(zl == ZL - 1, c == 1)
    far_y = jnp.where(special, wrap(y + 1, NY), y)

    def s2_peer(step, at_y):
        dh, dl, dc = step
        return place(x, wrap(zh + dh, ZH), wrap(c + dc, NC), at_y, wrap(zl + dl, ZL))

    s3_peers = [place(x, zh, c, wrap(y + dy, NY), zl) for dy in range(1, NY)]
    s4_peers = [place(wrap(x + dx, NX), zh, c, y, zl) for dx in range(1, NX)]
    sibling = place(x, zh, 1 - c, y, zl)

    barrier = pltpu.get_barrier_semaphore()
    greeted = ring + s1_peers + s3_peers
    greeted += [s2_peer(step, y) for step in s2_steps[1:]]
    expected = len(greeted)
    before_y = wrap(y + NY - 1, NY)
    greeted += [place(x, h, 1, before_y, ZL - 1) for h in range(ZH)]
    for peer in greeted:
        pl.semaphore_signal(barrier, inc=1, device_id=peer, device_id_type=MESH)

    def remote(src, dst, send, recv, peer):
        return pltpu.make_async_remote_copy(
            src_ref=src, dst_ref=dst, send_sem=send, recv_sem=recv, device_id=peer, device_id_type=MESH
        )

    lane = lax.broadcasted_iota(jnp.int32, (1, CHUNK), 1)
    for to in (0, 2):
        ids[to] = jnp.full(ids.shape[1:], -1, jnp.int32)
    for load in loads[:5]:
        load.wait()
    for s, to in ((1, 2), (0, 0)):
        live_count = counts[s]
        for n, table in enumerate((src_ids, dst_ids, rel_ids, neg_ids)):
            for q in range(chunks):
                width = CHUNK if q < chunks - 1 else tail
                row = table[s : s + 1, q * CHUNK : q * CHUNK + width]
                if n == 2:
                    row = jnp.bitwise_and(row - 8 * j, rel_count - 1)
                    row = jnp.where(lane[:, :width] + q * CHUNK < live_count, row, -1)
                ids[to, q, n : n + 1, 0:width] = row
    loads[5].wait()
    src_t[0] = source_emb[...].astype(BF16)

    pl.semaphore_wait(barrier, jnp.where(special, expected + ZH * ZL * NC, expected))
    give_ids = remote(ids.at[2], ids.at[1], x_send.at[0], x_recv.at[0], ring[0])
    give_src = remote(src_t.at[0], src_t.at[1], x_send.at[1], x_recv.at[1], ring[2])
    give_ids.start()
    give_src.start()
    for load in loads[6:]:
        load.wait()

    dst_t[...] = dest_emb[...].astype(BF16)
    for start, width in blocks:
        block = dest_emb[start : start + width, :]
        if width < LANES:
            block = jnp.concatenate([block, jnp.zeros((LANES - width, LANES), F32)], axis=0)
        dst_n[:, start : start + width] = block.T[:, :width].astype(BF16)

    row = lax.broadcasted_iota(jnp.int32, (rel_count, LANES), 0)
    spot = lax.broadcasted_iota(jnp.int32, (rel_count, LANES), 1)
    chosen = jnp.logical_and(row == jnp.bitwise_and(spot + 8 * j, rel_count - 1), spot < 16)
    rel_t[...] = nn(relations[...].astype(BF16), jnp.where(chosen, 1.0, 0.0).astype(BF16)).astype(BF16)

    iota = lax.broadcasted_iota(jnp.int32, (LANES, CHUNK), 0)

    def count_rows(s):
        seen = jnp.zeros((LANES, CHUNK), F32)
        for q in range(chunks):
            seen = seen + jnp.where(iota == ids[s, q, 3:4, :], 1.0, 0.0)
        count_b[s] = jnp.broadcast_to(jnp.sum(seen, axis=1, keepdims=True), (LANES, CHUNK))

    rel_sum[...] = jnp.zeros(rel_sum.shape, F32)
    src_sum[...] = jnp.zeros(src_sum.shape, F32)
    dst_sum[...] = jnp.zeros(dst_sum.shape, F32)

    def first_pass(s):
        def body(local, carry):
            q = s * chunks + local
            rows = ids[s, local]
            one_src = jnp.where(iota == rows[0:1], 1.0, 0.0).astype(BF16)
            hit_dst = iota == rows[1:2]
            one_rel = jnp.where(iota == rows[2:3], 1.0, 0.0).astype(BF16)
            a = nn(src_t[s], one_src)
            r = nn(rel_t[...], one_rel)
            a_re, a_im, r_re, r_im = a[:half], a[half:], r[:half], r[half:]
            query = jnp.concatenate([a_re * r_re - a_im * r_im, a_re * r_im + a_im * r_re], axis=0)
            query_high, query_low = split2(query)
            scores = nn(dst_n[...], query_high)
            rest = nn(dst_n[...], query_low)
            positive = jnp.sum(jnp.where(hit_dst, scores + rest, 0.0), axis=0, keepdims=True)
            seen = count_b[s]
            scores = jnp.where(seen > 0.0, scores, ABSENT)
            peak = jnp.maximum(jnp.max(scores, axis=0, keepdims=True), positive)
            pos_weight = jnp.exp(positive - peak)
            neg_weight = jnp.exp(scores - peak)
            partition = pos_weight + jnp.sum(neg_weight * seen, axis=0, keepdims=True)
            pos_coeff = pos_weight / partition - 1.0
            neg_coeff = (neg_weight * (1.0 / partition)).astype(BF16).astype(F32)
            pos_part = jnp.where(hit_dst, pos_coeff, 0.0)
            weight_high, weight_low = split2(neg_coeff * seen + pos_part)
            query_s[q, 0] = query_high
            query_s[q, 1] = query_low
            weight_s[q, 0] = weight_high
            weight_s[q, 1] = weight_low
            weight_s[q, 2] = pos_part.astype(BF16)
            table = dst_t[...]
            g = nn(
                jnp.concatenate([table, table], axis=1),
                jnp.concatenate([weight_high, weight_low], axis=0),
            )
            g_re, g_im = g[:half], g[half:]
            rel_grad = jnp.concatenate([g_re * a_re + g_im * a_im, g_im * a_re - g_re * a_im], axis=0)
            rel_high, rel_low = split2(rel_grad)
            rel_sum[0:emb, :] += nt(rel_high, one_rel) + nt(rel_low, one_rel)
            src_grad = jnp.concatenate([g_re * r_re + g_im * r_im, g_im * r_re - g_re * r_im], axis=0)
            src_high, src_low = split2(src_grad)
            grad_s[q, 0] = src_high
            grad_s[q, 1] = src_low
            return carry

        lax.fori_loop(0, chunks, body, 0)

    def second_pass(s):
        def body(local, carry):
            q = s * chunks + local
            rows = ids[s, local]
            one_src = jnp.where(iota == rows[0:1], 1.0, 0.0).astype(BF16)
            src_sum[s] += nt(grad_s[q, 0], one_src) + nt(grad_s[q, 1], one_src)
            dst_sum[...] += (
                nt(query_s[q, 0], weight_s[q, 0])
                + nt(query_s[q, 0], weight_s[q, 1])
                + nt(query_s[q, 1], weight_s[q, 2])
            )
            return carry

        lax.fori_loop(0, chunks, body, 0)

    count_rows(0)
    first_pass(0)
    second_pass(0)
    give_ids.wait()
    give_src.wait()
    count_rows(1)
    first_pass(1)

    for b in range(NX):
        block = rel_sum[b * LANES : (b + 1) * LANES, :].T
        for rows in range(NC):
            part[b, rows] = block[8 * rows : 8 * rows + 8, :]
    s1 = [
        remote(
            part.at[wrap(x + dx, NX), wrap(c + dc, NC)],
            part_in.at[n],
            s1_send.at[n],
            s1_recv.at[n],
            s1_peers[n],
        )
        for n, (dx, dc) in enumerate(s1_steps)
    ]
    for copy in s1:
        copy.start()

    second_pass(1)
    back_out[...] = src_sum[1].astype(BF16)
    back = remote(back_out, back_in, b_send.at[0], b_recv.at[0], ring[3])
    back.start()

    tile = part[x, c]
    for n, copy in enumerate(s1):
        copy.wait()
        tile = tile + part_in[n]
    mine[...] = tile

    s2 = [
        remote(mine, column.at[zh, zl, c], s2_send.at[n], s2_recv.at[n], s2_peer(step, far_y))
        for n, step in enumerate(s2_steps)
    ]
    for copy in s2[1:]:
        copy.start()

    @pl.when(special)
    def _():
        s2[0].start()

    @pl.when(jnp.logical_not(special))
    def _():
        column[zh, zl, c] = mine[...]

    for copy in s2[1:]:
        copy.wait()

    @pl.when(special)
    def _():
        s2[0].wait()

    firsts = [column[0, l, 0] + column[1, l, 0] for l in range(ZL)]
    lasts = [column[0, l, 1] + column[1, l, 1] for l in range(ZL)]
    whole = [firsts[l] + lasts[(l + ZL - 1) % ZL] for l in range(ZL)]
    for n in range(2):
        full[x, y, c, n] = jnp.where(c == 0, whole[n], whole[2 + n])
    order = sorted(range(NY), key=lambda dy: (min(dy, NY - dy), dy))
    s3 = {
        dy: remote(full.at[x, y, c], full.at[x, y, c], s3_send.at[dy], s3_recv.at[dy], s3_peers[dy - 1])
        for dy in order
        if dy
    }
    for dy in order[1:]:
        s3[dy].start()

    def s4_copies(dy):
        at = full.at[x, wrap(y + NY - dy, NY), c]
        return [
            remote(at, at, s4_send.at[dy, n], s4_recv.at[dy, n], s4_peers[n]) for n in range(NX - 1)
        ]

    def s5_copy(dy):
        at = full.at[:, wrap(y + NY - dy, NY), c]
        return remote(at, at, s5_send.at[dy], s5_recv.at[dy], sibling)

    s4 = {dy: s4_copies(dy) for dy in order}
    s5 = {dy: s5_copy(dy) for dy in order}
    for copy in s4[0]:
        copy.start()

    def update(total, table, acc, out, new_acc):
        accum = acc[...] + jnp.sum(total * total, axis=0, keepdims=True) * (1.0 / emb)
        new_acc[...] = accum
        out[...] = table[...] - total * (learn_rate / jnp.sqrt(accum))

    update(dst_sum[...], dest_emb, dest_acc, new_dest, new_dest_acc)
    back.wait()
    update(src_sum[0] + back_in[...].astype(F32), source_emb, source_acc, new_source, new_source_acc)

    def to_sibling(dy):
        for copy in s4[dy]:
            copy.wait_recv()
        s5[dy].start()

    lag = 3
    for n, dy in enumerate(order):
        if dy:
            s3[dy].wait_recv()
            for copy in s4[dy]:
                copy.start()
        if n >= lag:
            to_sibling(order[n - lag])
    for dy in order[max(0, NY - lag) :]:
        to_sibling(dy)
    for dy in order:
        s5[dy].wait_recv()

    wide = min(LANES, rel_count)
    for h in range(rel_count // wide):
        at = slice(h * wide, (h + 1) * wide)
        tiles = [full[b].reshape(rel_count, LANES)[at].T[:width] for b, (start, width) in enumerate(blocks)]
        squares = sum(jnp.sum(tile * tile, axis=0, keepdims=True) for tile in tiles)
        accum = rel_acc[0:1, at] + squares * (1.0 / emb)
        new_rel_acc[0:1, at] = accum
        scale = learn_rate / jnp.sqrt(accum)
        for tile, (start, width) in zip(tiles, blocks):
            new_relations[start : start + width, at] = relations[start : start + width, at] - tile * scale

    for dy in order:
        if dy:
            s3[dy].wait_send()
        for copy in s4[dy]:
            copy.wait_send()
        s5[dy].wait_send()


def write_out(*refs):
    count = (len(refs) - 1) // 2
    sem = refs[-1]
    copies = [pltpu.make_async_copy(refs[n], refs[count + n], sem.at[n]) for n in range(count)]
    for copy in copies:
        copy.start()
    for copy in copies:
        copy.wait()


def solution(mesh):
    n_src, n_dst = mesh.shape["src"], mesh.shape["dst"]
    NX, NY = n_src // (ZH * NC), n_dst // ZL

    def shards(
        source_emb,
        dest_emb,
        source_acc,
        dest_acc,
        relations,
        rel_acc,
        src_ids,
        dst_ids,
        rel_ids,
        neg_ids,
        counts,
    ):
        rows, emb = source_emb.shape
        rel_count = relations.shape[0]
        slots = src_ids.shape[3]
        chunks = pl.cdiv(slots, CHUNK)
        hbm = pl.BlockSpec(memory_space=pl.ANY)
        vmem = pl.BlockSpec(memory_space=pltpu.VMEM)
        dma = pltpu.SemaphoreType.DMA
        outs = pl.pallas_call(
            functools.partial(kernel, NX, NY),
            out_shape=(
                pltpu.VMEM((emb, rows), F32),
                pltpu.VMEM((emb, rows), F32),
                pltpu.VMEM((1, rows), F32),
                pltpu.VMEM((1, rows), F32),
                pltpu.VMEM((emb, rel_count), F32),
                pltpu.VMEM((1, rel_count), F32),
            ),
            in_specs=[hbm] * 11,
            out_specs=[vmem] * 6,
            scratch_shapes=[
                pltpu.SMEM((2,), jnp.int32),
                pltpu.VMEM((emb, rows), F32),
                pltpu.VMEM((emb, rows), F32),
                pltpu.VMEM((1, rows), F32),
                pltpu.VMEM((1, rows), F32),
                pltpu.VMEM((emb, rel_count), F32),
                pltpu.VMEM((1, rel_count), F32),
                pltpu.VMEM((2, slots), jnp.int32),
                pltpu.VMEM((2, slots), jnp.int32),
                pltpu.VMEM((2, slots), jnp.int32),
                pltpu.VMEM((2, slots), jnp.int32),
                pltpu.VMEM((3, chunks, 4, CHUNK), jnp.int32),
                pltpu.VMEM((2, emb, LANES), BF16),
                pltpu.VMEM((emb, LANES), BF16),
                pltpu.VMEM((LANES, emb), BF16),
                pltpu.VMEM((emb, LANES), BF16),
                pltpu.VMEM((2, LANES, CHUNK), F32),
                pltpu.VMEM((2 * chunks, 2, emb, CHUNK), BF16),
                pltpu.VMEM((2 * chunks, 3, LANES, CHUNK), BF16),
                pltpu.VMEM((2 * chunks, 2, emb, CHUNK), BF16),
                pltpu.VMEM((NX * LANES, LANES), F32),
                pltpu.VMEM((2, emb, LANES), F32),
                pltpu.VMEM((emb, LANES), F32),
                pltpu.VMEM((emb, LANES), BF16),
                pltpu.VMEM((emb, LANES), BF16),
                pltpu.VMEM((NX, NC, 8, LANES), F32),
                pltpu.VMEM((NX * NC - 1, 8, LANES), F32),
                pltpu.VMEM((8, LANES), F32),
                pltpu.VMEM((ZH, ZL, NC, 8, LANES), F32),
                pltpu.VMEM((NX, NY, NC, ZL // NC, 8, LANES), F32),
                dma((11,)),
                dma((2,)),
                dma((2,)),
                dma((1,)),
                dma((1,)),
                dma((NX * NC - 1,)),
                dma((NX * NC - 1,)),
                dma((ZH * ZL * NC,)),
                dma((ZH * ZL * NC,)),
                dma((NY,)),
                dma((NY,)),
                dma((NY, NX - 1)),
                dma((NY, NX - 1)),
                dma((NY,)),
                dma((NY,)),
            ],
            compiler_params=pltpu.CompilerParams(
                collective_id=0, has_side_effects=True, vmem_limit_bytes=40 * 2**20
            ),
            cost_estimate=pl.CostEstimate(flops=4 * 10**9, bytes_accessed=3 * 10**6, transcendentals=3 * 10**5),
            name="bucket_round",
        )(
            *(
                pltpu.with_memory_space_constraint(value, pltpu.HBM)
                for value in (
                    counts.reshape(2),
                    source_emb.T,
                    dest_emb.T,
                    source_acc.reshape(1, rows),
                    dest_acc.reshape(1, rows),
                    relations.T,
                    rel_acc.reshape(1, rel_count),
                    src_ids.reshape(2, slots),
                    dst_ids.reshape(2, slots),
                    rel_ids.reshape(2, slots),
                    neg_ids.reshape(2, slots),
                )
            )
        )
        outs = pl.pallas_call(
            write_out,
            out_shape=tuple(pltpu.HBM(out.shape, out.dtype) for out in outs),
            in_specs=[vmem] * 6,
            out_specs=[hbm] * 6,
            scratch_shapes=[dma((6,))],
            name="write_out",
        )(*(pltpu.with_memory_space_constraint(out, pltpu.VMEM) for out in outs))
        new_source, new_dest, new_source_acc, new_dest_acc, new_relations, new_rel_acc = outs
        return (
            new_source.T,
            new_dest.T,
            new_source_acc.reshape(rows),
            new_dest_acc.reshape(rows),
            new_relations.T,
            new_rel_acc.reshape(rel_count),
        )

    rows_spec = P(("src", "dst"), None)
    row_spec = P(("src", "dst"))
    ids_spec = P("src", "dst", None, None)
    return jax.shard_map(
        shards,
        mesh=mesh,
        in_specs=(rows_spec, rows_spec, row_spec, row_spec, P(), P())
        + (ids_spec,) * 4
        + (P("src", "dst", None),),
        out_specs=(rows_spec, rows_spec, row_spec, row_spec, P(), P()),
        check_vma=False,
    )
```

time: 58.3 us -> 52.3 us (0.90)
  local copies, waits for them, and re-layouts: 6.09 us -> 0 us
    unnamed x29 -> x0, local copies, waits for them, and re-layouts: 6.09 us -> none
    pallas_call x1 -> x2, Pallas kernels: 51.2 us -> 51.6 us  [the longest x1 50.6 us: shards(): pl.pallas_call(functools.partial(kernel, NX, NY), out_shape=(pltpu.VMEM((...]
where the time goes in v2:
time: 52.3 us; the launch traced here: 52.2 us
  Pallas kernels  51.6 us (99%)
  between operations  0.64 us (1%)
    pallas_call x1, Pallas kernels, shards(): pl.pallas_call(functools.partial(kernel, NX, NY), out_shape=(pltpu.VMEM((...  50.6 us

profile of v2, /device:TPU:1, one launch (start us, length us, event | category | flops | bytes accessed | tf_op | source)
XLA Modules:
  0.0 52.2 jit_solution(17746282398053662040)
XLA Ops:
  0.6 50.6 %bucket_round.1 = (f32[400,128]{1,0:T(8,128)S(1)}, f32[400,128]{1,0:T(8,128)S(1)}, f32[1,128]{1,0:T(1,128)S(1)}, f32[1,128]{1,0:T(1,128)S(1)}, f32[400,256]{1,0:T(8,128)S(1)}, /*index=5*/f32[1,256]{1,0:T(1,128)S(1)}) custom-call(s32[2]{0:T(128)} %bitcast.29, f32[400,128]{1,0:T(8,128)} %bitcast.19, f32[400,128]{1,0:T(8,128)} %bitcast.20, f32[1,128]{1,0:T(1,128)} %bitcast.30, ...), custom_call_target="tpu_custom_call" | custom-call | flops 4000000000 | bytes 3000000 | tf_op jit(solution)/shard_map/bucket_round/pallas_call | solution.py:452
  51.2 1.0 %write_out.1 = (f32[400,128]{1,0:T(8,128)}, f32[400,128]{1,0:T(8,128)}, f32[1,128]{1,0:T(1,128)}, f32[1,128]{1,0:T(1,128)}, f32[400,256]{1,0:T(8,128)}, /*index=5*/f32[1,256]{1,0:T(1,128)}) custom-call(f32[400,128]{1,0:T(8,128)S(1)} %get-tuple-element.18.refs_0_, f32[400,128]{1,0:T(8,128)S(1)} %get-tuple-element.19.refs_1_, ...), custom_call_target="tpu_custom_call" | custom-call | tf_op jit(solution)/shard_map/write_out/pallas_call | solution.py:534

commit v3 on v2

--- a/solution.py
+++ b/solution.py
@@ -116,8 +116,6 @@
             )
         )
     ]
-    for load in loads:
-        load.start()
 
     emb = source_emb.shape[0]
     half = emb // 2
@@ -162,8 +160,11 @@
     expected = len(greeted)
     before_y = wrap(y + NY - 1, NY)
     greeted += [place(x, h, 1, before_y, ZL - 1) for h in range(ZH)]
-    for peer in greeted:
+    for n, peer in enumerate(greeted):
         pl.semaphore_signal(barrier, inc=1, device_id=peer, device_id_type=MESH)
+        if n == len(ring) - 1:
+            for load in loads:
+                load.start()
 
     def remote(src, dst, send, recv, peer):
         return pltpu.make_async_remote_copy(
@@ -265,7 +266,7 @@
             grad_s[q, 1] = src_low
             return carry
 
-        lax.fori_loop(0, chunks, body, 0)
+        lax.fori_loop(0, chunks, body, 0, unroll=True)
 
     def second_pass(s):
         def body(local, carry):
@@ -280,14 +281,14 @@
             )
             return carry
 
-        lax.fori_loop(0, chunks, body, 0)
+        lax.fori_loop(0, chunks, body, 0, unroll=True)
 
     count_rows(0)
     first_pass(0)
     second_pass(0)
     give_ids.wait()
+    count_rows(1)
     give_src.wait()
-    count_rows(1)
     first_pass(1)
 
     for b in range(NX):
@@ -310,7 +311,6 @@
     second_pass(1)
     back_out[...] = src_sum[1].astype(BF16)
     back = remote(back_out, back_in, b_send.at[0], b_recv.at[0], ring[3])
-    back.start()
 
     tile = part[x, c]
     for n, copy in enumerate(s1):
@@ -322,7 +322,7 @@
         remote(mine, column.at[zh, zl, c], s2_send.at[n], s2_recv.at[n], s2_peer(step, far_y))
         for n, step in enumerate(s2_steps)
     ]
-    for copy in s2[1:]:
+    for copy in s2[:0:-1]:
         copy.start()
 
     @pl.when(special)
@@ -343,31 +343,31 @@
     firsts = [column[0, l, 0] + column[1, l, 0] for l in range(ZL)]
     lasts = [column[0, l, 1] + column[1, l, 1] for l in range(ZL)]
     whole = [firsts[l] + lasts[(l + ZL - 1) % ZL] for l in range(ZL)]
+    order = sorted(range(NY), key=lambda dy: (min(dy, NY - dy), dy))
     for n in range(2):
-        full[x, y, c, n] = jnp.where(c == 0, whole[n], whole[2 + n])
-    order = sorted(range(NY), key=lambda dy: (min(dy, NY - dy), dy))
-    s3 = {
-        dy: remote(full.at[x, y, c], full.at[x, y, c], s3_send.at[dy], s3_recv.at[dy], s3_peers[dy - 1])
-        for dy in order
-        if dy
-    }
-    for dy in order[1:]:
-        s3[dy].start()
-
-    def s4_copies(dy):
-        at = full.at[x, wrap(y + NY - dy, NY), c]
-        return [
-            remote(at, at, s4_send.at[dy, n], s4_recv.at[dy, n], s4_peers[n]) for n in range(NX - 1)
-        ]
-
-    def s5_copy(dy):
-        at = full.at[:, wrap(y + NY - dy, NY), c]
-        return remote(at, at, s5_send.at[dy], s5_recv.at[dy], sibling)
-
-    s4 = {dy: s4_copies(dy) for dy in order}
-    s5 = {dy: s5_copy(dy) for dy in order}
+        full[x, 0, c, n] = jnp.where(c == 0, whole[n], whole[2 + n])
+    s3 = [
+        remote(full.at[x, 0, c], full.at[x, n, c], s3_send.at[n], s3_recv.at[n], s3_peers[order[n] - 1])
+        for n in range(1, NY)
+    ]
+    for copy in s3[::-1]:
+        copy.start()
+    cuts = [0] + list(range(1, NY, 2)) + [NY]
+    groups = [slice(a, b) for a, b in zip(cuts, cuts[1:])]
+
+    def s4_copies(g):
+        at = full.at[x, groups[g], c]
+        return [remote(at, at, s4_send.at[g, n], s4_recv.at[g, n], s4_peers[n]) for n in range(NX - 1)]
+
+    def s5_copy(g):
+        at = full.at[:, groups[g], c]
+        return remote(at, at, s5_send.at[g], s5_recv.at[g], sibling)
+
+    s4 = [s4_copies(g) for g in range(len(groups))]
+    s5 = [s5_copy(g) for g in range(len(groups))]
     for copy in s4[0]:
         copy.start()
+    back.start()
 
     def update(total, table, acc, out, new_acc):
         accum = acc[...] + jnp.sum(total * total, axis=0, keepdims=True) * (1.0 / emb)
@@ -375,31 +375,37 @@
         out[...] = table[...] - total * (learn_rate / jnp.sqrt(accum))
 
     update(dst_sum[...], dest_emb, dest_acc, new_dest, new_dest_acc)
+
+    def to_sibling(g):
+        for copy in s4[g]:
+            copy.wait_recv()
+        s5[g].start()
+
+    for g in range(1, len(groups)):
+        for n in range(groups[g].start, groups[g].stop):
+            s3[n - 1].wait_recv()
+        for copy in s4[g]:
+            copy.start()
+        if g >= 2:
+            to_sibling(g - 2)
     back.wait()
     update(src_sum[0] + back_in[...].astype(F32), source_emb, source_acc, new_source, new_source_acc)
-
-    def to_sibling(dy):
-        for copy in s4[dy]:
-            copy.wait_recv()
-        s5[dy].start()
-
-    lag = 3
-    for n, dy in enumerate(order):
-        if dy:
-            s3[dy].wait_recv()
-            for copy in s4[dy]:
-                copy.start()
-        if n >= lag:
-            to_sibling(order[n - lag])
-    for dy in order[max(0, NY - lag) :]:
-        to_sibling(dy)
-    for dy in order:
-        s5[dy].wait_recv()
+    for g in range(max(0, len(groups) - 2), len(groups)):
+        to_sibling(g)
+    for copy in s5:
+        copy.wait_recv()
 
     wide = min(LANES, rel_count)
     for h in range(rel_count // wide):
         at = slice(h * wide, (h + 1) * wide)
-        tiles = [full[b].reshape(rel_count, LANES)[at].T[:width] for b, (start, width) in enumerate(blocks)]
+        tiles = []
+        for b, (start, width) in enumerate(blocks):
+            rows = []
+            for t in range(wide // (8 * ZL)):
+                steps = wrap(y + NY - (h * (wide // (8 * ZL)) + t), NY)
+                spot = jnp.where(steps <= NY // 2, jnp.maximum(2 * steps - 1, 0), 2 * (NY - steps))
+                rows.append(full[b, spot].reshape(8 * ZL, LANES))
+            tiles.append(jnp.concatenate(rows, axis=0).T[:width])
         squares = sum(jnp.sum(tile * tile, axis=0, keepdims=True) for tile in tiles)
         accum = rel_acc[0:1, at] + squares * (1.0 / emb)
         new_rel_acc[0:1, at] = accum
@@ -407,12 +413,12 @@
         for tile, (start, width) in zip(tiles, blocks):
             new_relations[start : start + width, at] = relations[start : start + width, at] - tile * scale
 
-    for dy in order:
-        if dy:
-            s3[dy].wait_send()
-        for copy in s4[dy]:
+    for copy in s3:
+        copy.wait_send()
+    for g in range(len(groups)):
+        for copy in s4[g]:
             copy.wait_send()
-        s5[dy].wait_send()
+        s5[g].wait_send()
 
 
 def write_out(*refs):

time: 52.3 us -> 49.9 us (0.954)
  Pallas kernels: 51.6 us -> 49.1 us
    pallas_call x1, Pallas kernels: 50.6 us -> 48.2 us  [shards(): pl.pallas_call(functools.partial(kernel, NX, NY), out_shape=(pltpu.VMEM((...]
where the time goes in v3:
time: 49.9 us; the launch traced here: 49.8 us
  Pallas kernels  49.1 us (98%)
  between operations  0.64 us (1%)
    pallas_call x1, Pallas kernels, shards(): pl.pallas_call(functools.partial(kernel, NX, NY), out_shape=(pltpu.VMEM((...  48.2 us

profile of v3, /device:TPU:1, one launch (start us, length us, event | category | flops | bytes accessed | tf_op | source)
XLA Modules:
  0.0 49.8 jit_solution(15300178918287814959)
XLA Ops:
  0.6 48.2 %bucket_round.1 = (f32[400,128]{1,0:T(8,128)S(1)}, f32[400,128]{1,0:T(8,128)S(1)}, f32[1,128]{1,0:T(1,128)S(1)}, f32[1,128]{1,0:T(1,128)S(1)}, f32[400,256]{1,0:T(8,128)S(1)}, /*index=5*/f32[1,256]{1,0:T(1,128)S(1)}) custom-call(s32[2]{0:T(128)} %bitcast.29, f32[400,128]{1,0:T(8,128)} %bitcast.19, f32[400,128]{1,0:T(8,128)} %bitcast.20, f32[1,128]{1,0:T(1,128)} %bitcast.30, ...), custom_call_target="tpu_custom_call" | custom-call | flops 4000000000 | bytes 3000000 | tf_op jit(solution)/shard_map/bucket_round/pallas_call | solution.py:458
  48.8 1.0 %write_out.1 = (f32[400,128]{1,0:T(8,128)}, f32[400,128]{1,0:T(8,128)}, f32[1,128]{1,0:T(1,128)}, f32[1,128]{1,0:T(1,128)}, f32[400,256]{1,0:T(8,128)}, /*index=5*/f32[1,256]{1,0:T(1,128)}) custom-call(f32[400,128]{1,0:T(8,128)S(1)} %get-tuple-element.18.refs_0_, f32[400,128]{1,0:T(8,128)S(1)} %get-tuple-element.19.refs_1_, ...), custom_call_target="tpu_custom_call" | custom-call | tf_op jit(solution)/shard_map/write_out/pallas_call | solution.py:540

commit v4 on v3

--- a/solution.py
+++ b/solution.py
@@ -322,7 +322,7 @@
         remote(mine, column.at[zh, zl, c], s2_send.at[n], s2_recv.at[n], s2_peer(step, far_y))
         for n, step in enumerate(s2_steps)
     ]
-    for copy in s2[:0:-1]:
+    for copy in s2[1:]:
         copy.start()
 
     @pl.when(special)
@@ -350,9 +350,9 @@
         remote(full.at[x, 0, c], full.at[x, n, c], s3_send.at[n], s3_recv.at[n], s3_peers[order[n] - 1])
         for n in range(1, NY)
     ]
-    for copy in s3[::-1]:
+    for copy in s3:
         copy.start()
-    cuts = [0] + list(range(1, NY, 2)) + [NY]
+    cuts = [0, 1, min(3, NY), min(5, NY), NY] if NY > 5 else [0, 1, NY]
     groups = [slice(a, b) for a, b in zip(cuts, cuts[1:])]
 
     def s4_copies(g):

time: 49.9 us -> 47.9 us (0.960)
  Pallas kernels: 49.1 us -> 47.1 us
    pallas_call x1, Pallas kernels: 48.2 us -> 46.2 us  [shards(): pl.pallas_call(functools.partial(kernel, NX, NY), out_shape=(pltpu.VMEM((...]
where the time goes in v4:
time: 47.9 us; the launch traced here: 47.8 us
  Pallas kernels  47.1 us (98%)
  between operations  0.64 us (1%)
    pallas_call x1, Pallas kernels, shards(): pl.pallas_call(functools.partial(kernel, NX, NY), out_shape=(pltpu.VMEM((...  46.2 us

profile of v4, /device:TPU:1, one launch (start us, length us, event | category | flops | bytes accessed | tf_op | source)
XLA Modules:
  0.0 47.8 jit_solution(16378491927940243402)
XLA Ops:
  0.6 46.2 %bucket_round.1 = (f32[400,128]{1,0:T(8,128)S(1)}, f32[400,128]{1,0:T(8,128)S(1)}, f32[1,128]{1,0:T(1,128)S(1)}, f32[1,128]{1,0:T(1,128)S(1)}, f32[400,256]{1,0:T(8,128)S(1)}, /*index=5*/f32[1,256]{1,0:T(1,128)S(1)}) custom-call(s32[2]{0:T(128)} %bitcast.29, f32[400,128]{1,0:T(8,128)} %bitcast.19, f32[400,128]{1,0:T(8,128)} %bitcast.20, f32[1,128]{1,0:T(1,128)} %bitcast.30, ...), custom_call_target="tpu_custom_call" | custom-call | flops 4000000000 | bytes 3000000 | tf_op jit(solution)/shard_map/bucket_round/pallas_call | solution.py:458
  46.8 1.0 %write_out.1 = (f32[400,128]{1,0:T(8,128)}, f32[400,128]{1,0:T(8,128)}, f32[1,128]{1,0:T(1,128)}, f32[1,128]{1,0:T(1,128)}, f32[400,256]{1,0:T(8,128)}, /*index=5*/f32[1,256]{1,0:T(1,128)}) custom-call(f32[400,128]{1,0:T(8,128)S(1)} %get-tuple-element.18.refs_0_, f32[400,128]{1,0:T(8,128)S(1)} %get-tuple-element.19.refs_1_, ...), custom_call_target="tpu_custom_call" | custom-call | tf_op jit(solution)/shard_map/write_out/pallas_call | solution.py:540

commit v5 on v4

--- a/solution.py
+++ b/solution.py
@@ -260,10 +260,7 @@
             rel_grad = jnp.concatenate([g_re * a_re + g_im * a_im, g_im * a_re - g_re * a_im], axis=0)
             rel_high, rel_low = split2(rel_grad)
             rel_sum[0:emb, :] += nt(rel_high, one_rel) + nt(rel_low, one_rel)
-            src_grad = jnp.concatenate([g_re * r_re + g_im * r_im, g_im * r_re - g_re * r_im], axis=0)
-            src_high, src_low = split2(src_grad)
-            grad_s[q, 0] = src_high
-            grad_s[q, 1] = src_low
+            grad_s[q] = g
             return carry
 
         lax.fori_loop(0, chunks, body, 0, unroll=True)
@@ -273,7 +270,13 @@
             q = s * chunks + local
             rows = ids[s, local]
             one_src = jnp.where(iota == rows[0:1], 1.0, 0.0).astype(BF16)
-            src_sum[s] += nt(grad_s[q, 0], one_src) + nt(grad_s[q, 1], one_src)
+            one_rel = jnp.where(iota == rows[2:3], 1.0, 0.0).astype(BF16)
+            r = nn(rel_t[...], one_rel)
+            g = grad_s[q]
+            g_re, g_im, r_re, r_im = g[:half], g[half:], r[:half], r[half:]
+            src_grad = jnp.concatenate([g_re * r_re + g_im * r_im, g_im * r_re - g_re * r_im], axis=0)
+            src_high, src_low = split2(src_grad)
+            src_sum[s] += nt(src_high, one_src) + nt(src_low, one_src)
             dst_sum[...] += (
                 nt(query_s[q, 0], weight_s[q, 0])
                 + nt(query_s[q, 0], weight_s[q, 1])
@@ -487,7 +490,7 @@
                 pltpu.VMEM((2, LANES, CHUNK), F32),
                 pltpu.VMEM((2 * chunks, 2, emb, CHUNK), BF16),
                 pltpu.VMEM((2 * chunks, 3, LANES, CHUNK), BF16),
-                pltpu.VMEM((2 * chunks, 2, emb, CHUNK), BF16),
+                pltpu.VMEM((2 * chunks, emb, CHUNK), F32),
                 pltpu.VMEM((NX * LANES, LANES), F32),
                 pltpu.VMEM((2, emb, LANES), F32),
                 pltpu.VMEM((emb, LANES), F32),

time: 47.9 us -> 47.5 us (level)
  no operation moved by 1% of the time
where the time goes in v5:
time: 47.5 us; the launch traced here: 47.4 us
  Pallas kernels  46.7 us (98%)
  between operations  0.64 us (1%)
    pallas_call x1, Pallas kernels, shards(): pl.pallas_call(functools.partial(kernel, NX, NY), out_shape=(pltpu.VMEM((...  45.8 us
    pallas_call x1, Pallas kernels, shards(): pl.pallas_call(write_out, out_shape=tuple((pltpu.HBM(out.shape, out.dtype...  0.95 us

profile of v5, /device:TPU:1, one launch (start us, length us, event | category | flops | bytes accessed | tf_op | source)
XLA Modules:
  0.0 47.4 jit_solution(1553886962859525809)
XLA Ops:
  0.6 45.8 %bucket_round.1 = (f32[400,128]{1,0:T(8,128)S(1)}, f32[400,128]{1,0:T(8,128)S(1)}, f32[1,128]{1,0:T(1,128)S(1)}, f32[1,128]{1,0:T(1,128)S(1)}, f32[400,256]{1,0:T(8,128)S(1)}, /*index=5*/f32[1,256]{1,0:T(1,128)S(1)}) custom-call(s32[2]{0:T(128)} %bitcast.29, f32[400,128]{1,0:T(8,128)} %bitcast.19, f32[400,128]{1,0:T(8,128)} %bitcast.20, f32[1,128]{1,0:T(1,128)} %bitcast.30, ...), custom_call_target="tpu_custom_call" | custom-call | flops 4000000000 | bytes 3000000 | tf_op jit(solution)/shard_map/bucket_round/pallas_call | solution.py:461
  46.4 1.0 %write_out.1 = (f32[400,128]{1,0:T(8,128)}, f32[400,128]{1,0:T(8,128)}, f32[1,128]{1,0:T(1,128)}, f32[1,128]{1,0:T(1,128)}, f32[400,256]{1,0:T(8,128)}, /*index=5*/f32[1,256]{1,0:T(1,128)}) custom-call(f32[400,128]{1,0:T(8,128)S(1)} %get-tuple-element.18.refs_0_, f32[400,128]{1,0:T(8,128)S(1)} %get-tuple-element.19.refs_1_, ...), custom_call_target="tpu_custom_call" | custom-call | tf_op jit(solution)/shard_map/write_out/pallas_call | solution.py:543
